TPU v7x, 256 devices: a whole 4x4x8 slice. The times are simulated.
256 devices in a mesh: seq: 32 (over y, z_hi, core), mp: 8 (over z_lo, x).
Axes of the slice: x: 4, y: 4, z: 8 (z_hi: 4, z_lo: 2; z = z_hi * 2 + z_lo), core: 2. Of those that a mesh axis runs over, the one named last changes fastest.
Arguments:
- frames_in: bfloat16 [5632, 1536], P(('seq', 'mp')), may hold values from -6 to 6
- attn_gain: float32 [1536], replicated, may hold values from 0.25 to 1.75
- attn_shift: float32 [1536], replicated, may hold values from -3 to 3
- w_qkv: bfloat16 [3, 1536, 1536], P(None, 'mp'), may hold values from -0.76546554 to 0.76546554
- w_attn_out: bfloat16 [1536, 1536], P('mp'), may hold values from -2.5 to 2.5
- conv_gain: float32 [1536], replicated, may hold values from 0.25 to 1.75
- conv_shift: float32 [1536], replicated, may hold values from -3 to 3
- w_pointwise_in: bfloat16 [2, 1536, 1536], P(None, 'mp'), may hold values from -0.15625 to 0.15625
- depth_kernel: float32 [31, 1536], P(None, 'mp'), may hold values from -2 to 2
- norm_scale: float32 [1536], P('mp'), may hold values from 0.5 to 2
- norm_offset: float32 [1536], P('mp'), may hold values from -3 to 3
- w_pointwise_out: bfloat16 [1536, 1536], P('mp'), may hold values from -0.15625 to 0.15625
Outputs:
- block_out: bfloat16 [5632, 1536], P(('seq', 'mp'))
All inputs are finite; a program needn't handle non-finite values.
Results may differ from a plain program's by a relative error of at most 0.018.
The roundings to bfloat16 on the way count: a program that leaves them out, or rounds other values in their place, can miss the bound.
Values may be sent and summed in bfloat16 or wider, within the bound.
No kernel may reach another device: no remote copies, remote signals or barrier semaphores. Data moves between devices by JAX's collectives and lax.ppermute only.
A program may use at most 64 MiB of HBM per device.

v0:
```python
import jax
import jax.numpy as jnp
from jax import lax
from jax.sharding import PartitionSpec as P

D = 1536
HEADS = 16


def padded_2(cells, sides, width):
    for axis, dim in sides:
        count = lax.axis_size(axis)
        ends = count - 1
        head = lax.slice_in_dim(cells, 0, width, axis=dim)
        tail = lax.slice_in_dim(cells, cells.shape[dim] - width, cells.shape[dim], axis=dim)
        cells = jnp.concatenate(
            [
                lax.ppermute(tail, axis, [(i, (i + 1) % count) for i in range(ends)]),
                cells,
                lax.ppermute(head, axis, [((i + 1) % count, i) for i in range(ends)]),
            ],
            axis=dim,
        )
    return cells


def layer_norm(values, gain, shift):
    vf = values.astype(jnp.float32)
    center = vf - jnp.mean(vf, axis=-1, keepdims=True)
    spread = jnp.mean(center * center, axis=-1, keepdims=True)
    return (center * lax.rsqrt(spread + 1e-05) * gain + shift).astype(jnp.bfloat16)


def rotate(tensor, positions):
    half = tensor.shape[-1] // 2
    freq = 10000.0 ** (-jnp.arange(half).astype(jnp.float32) / half)
    angle = positions.astype(jnp.float32)[:, None] * freq[None, :]
    cosine = jnp.cos(angle)[:, None, :]
    sine = jnp.sin(angle)[:, None, :]
    first = tensor[..., :half]
    second = tensor[..., half:]
    return jnp.concatenate(
        [first * cosine - second * sine, first * sine + second * cosine], axis=-1
    )


def project_out_in(inputs, weight):
    return lax.dot_general(
        inputs, weight, (((1,), (1,)), ((), ())), preferred_element_type=jnp.float32
    )


def attend_block(carry, queries, key_block, value_block, scale):
    run_max, run_total, run_acc = carry
    scores = (
        jnp.einsum("qhd,khd->qhk", queries, key_block, preferred_element_type=jnp.float32) * scale
    )
    new_max = jnp.maximum(run_max, jnp.max(scores, axis=-1))
    weights = jnp.exp(scores - new_max[..., None])
    decay = jnp.exp(run_max - new_max)
    new_total = run_total * decay + jnp.sum(weights, axis=-1)
    mixed = jnp.einsum(
        "qhk,khd->qhd",
        weights.astype(jnp.bfloat16),
        value_block,
        preferred_element_type=jnp.float32,
    )
    return (new_max, new_total, run_acc * decay[..., None] + mixed)


def attend(carry, queries, key_piece, value_piece, scale):
    count = key_piece.shape[0]
    blocks = 1
    key_steps = key_piece.reshape(blocks, count // blocks, key_piece.shape[1], key_piece.shape[2])
    value_steps = value_piece.reshape(
        blocks, count // blocks, value_piece.shape[1], value_piece.shape[2]
    )

    def step(state, pair):
        return (attend_block(state, queries, pair[0], pair[1], scale), None)

    result, unused = lax.scan(step, carry, (key_steps, value_steps))
    return result


def local(
    frames_in,
    attn_gain,
    attn_shift,
    w_qkv,
    w_attn_out,
    conv_gain,
    conv_shift,
    w_pointwise_in,
    depth_kernel,
    norm_scale,
    norm_offset,
    w_pointwise_out,
):
    local_width = w_qkv.shape[1]
    local_heads = HEADS // lax.axis_size("mp")
    head_dim = D // HEADS
    scale = 1.0 / head_dim**0.5
    whole_in = lax.all_gather(frames_in, "mp", axis=0, tiled=True)
    frame_count = whole_in.shape[0]
    attn_in = layer_norm(whole_in, attn_gain, attn_shift)
    positions = lax.axis_index("seq") * frame_count + jnp.arange(frame_count)
    projected = [
        project_out_in(attn_in, w_qkv[slot]).reshape(frame_count, local_heads, head_dim)
        for slot in range(3)
    ]
    queries = rotate(projected[0], positions).astype(jnp.bfloat16)
    keys = rotate(projected[1], positions).astype(jnp.bfloat16)
    values = projected[2].astype(jnp.bfloat16)
    start_state = (
        jnp.full((frame_count, local_heads), -1e30, jnp.float32),
        jnp.zeros((frame_count, local_heads), jnp.float32),
        jnp.zeros((frame_count, local_heads, head_dim), jnp.float32),
    )
    run_max, run_total, run_acc = attend(
        start_state,
        queries,
        lax.all_gather(keys, "seq", axis=0, tiled=True),
        lax.all_gather(values, "seq", axis=0, tiled=True),
        scale,
    )
    context = (
        (run_acc / run_total[..., None]).astype(jnp.bfloat16).reshape(frame_count, local_width)
    )
    partial_attn = jnp.dot(context, w_attn_out, preferred_element_type=jnp.float32)
    attn_part = lax.psum_scatter(
        partial_attn.astype(jnp.bfloat16), "mp", scatter_dimension=0, tiled=True
    ).astype(jnp.float32)
    mid = (frames_in.astype(jnp.float32) + attn_part).astype(jnp.bfloat16)
    whole_mid = lax.all_gather(mid, "mp", axis=0, tiled=True)
    conv_in = layer_norm(whole_mid, conv_gain, conv_shift)
    value_half = project_out_in(conv_in, w_pointwise_in[0])
    gate_half = project_out_in(conv_in, w_pointwise_in[1])
    glu = (value_half * jax.nn.sigmoid(gate_half)).astype(jnp.bfloat16)
    taps = depth_kernel.shape[0]
    padded = padded_2(glu, (("seq", 0),), taps // 2)
    depth = jnp.zeros((frame_count, local_width), jnp.float32)
    for tap in range(taps):
        depth = depth + padded[tap : tap + frame_count].astype(jnp.float32) * depth_kernel[tap]
    normed = depth * norm_scale + norm_offset
    swish = (normed * jax.nn.sigmoid(normed)).astype(jnp.bfloat16)
    partial_conv = jnp.dot(swish, w_pointwise_out, preferred_element_type=jnp.float32)
    conv_part = lax.psum_scatter(
        partial_conv.astype(jnp.bfloat16), "mp", scatter_dimension=0, tiled=True
    ).astype(jnp.float32)
    return (mid.astype(jnp.float32) + conv_part).astype(jnp.bfloat16)


def solution(mesh):
    placed = (
        P(("seq", "mp"), None),
        P(),
        P(),
        P(None, "mp", None),
        P("mp", None),
        P(),
        P(),
        P(None, "mp", None),
        P(None, "mp"),
        P("mp"),
        P("mp"),
        P("mp", None),
    )
    return jax.shard_map(
        local, mesh=mesh, in_specs=placed, out_specs=P(("seq", "mp"), None), check_vma=False
    )
```

profile of v0, /device:TPU:56, one launch (start us, length us, event | category | flops | bytes accessed | tf_op | source)
XLA Modules:
  0.0 273.2 jit_solution(18006487947794246170)
XLA Ops:
  6.5 29.5 %all-gather = bf16[8,22,1536]{2,1,0:T(8,128)(2,1)S(1)} all-gather(bf16[1,22,1536]{2,1,0:T(8,128)(2,1)} %bitcast.74), channel_id=1, replica_groups=mesh['seq'=32,'mp'=8] {'mp'}, dimensions={0}, use_global_device_ids=true | all-gather | bytes 608256 | tf_op jit(solution)/shard_map/all_gather | solution.py:104
  36.7 1.5 fusion.65
  39.9 0.7 pad_maximum_fusion.2
  40.8 1.0 convolution_convert_fusion.2
  41.8 56.4 %all-gather.5.cloned.1.call-done = bf16[5632,2,96]{2,0,1:T(8,128)(2,1)} async-done(((bf16[176,2,96]{2,0,1:T(8,128)(2,1)}), bf16[5632,2,96]{2,0,1:T(8,128)(2,1)}) %all-gather.5.cloned.1.call-update) | async-done | bytes 2162704 | tf_op jit(solution)/shard_map/all_gather | solution.py:123
  98.2 3.1 %fusion.69 = (f32[176,2]{0,1:T(2,128)S(1)}, f32[176,2,5632]{2,0,1:T(8,128)S(1)}) fusion(bf16[5632,2,96]{2,0,1:T(8,128)(2,1)} %all-gather.5.cloned.1.call-done, bf16[176,2,48]{2,0,1:T(8,128)(2,1)S(1)} %get-tuple-element.28, bf16[176,2,48]{2,0,1:T(8,128)(2,1)S(1)} %get-tuple-element.20), kind=kOutput, calls=%fused_computation.138 | convolution fusion | flops 384732832 | bytes 10161536 | tf_op jit(solution)/shard_map/while/body/eval_jaxpr/qhd,khd->qhk/dot_general | solution.py:56
  101.4 1.2 fusion.3
  102.6 1.9 copy-done.1
  104.5 50.5 %all-gather.7.cloned.1.call-done = bf16[5632,2,96]{2,0,1:T(8,128)(2,1)} async-done(((bf16[176,2,96]{2,0,1:T(8,128)(2,1)}), bf16[5632,2,96]{2,0,1:T(8,128)(2,1)}) %all-gather.7.cloned.1.call-update) | async-done | bytes 2162704 | tf_op jit(solution)/shard_map/all_gather | solution.py:124
  154.9 5.4 %fusion.21 = bf16[176,2,96]{2,0,1:T(8,128)(2,1)S(1)} fusion(bf16[5632,2,96]{2,0,1:T(8,128)(2,1)} %all-gather.7.cloned.1.call-done, f32[176,2,5632]{2,0,1:T(8,128)} %copy-done.1, f32[176,2]{0,1:T(2,128)S(1)} %broadcast_maximum_fusion, f32[176,2]{0,1:T(2,128)S(1)} %get-tuple-element.69, f32[176,2]{0,1:T(2,128)S(1)} %get-tuple-element.68), kind=kOutput, calls=%fused_computation.19 | convolution fusion | flops 384699392 | bytes 10164352 | tf_op jit(solution)/shard_map/while/body/eval_jaxpr/qhk,khd->qhd/dot_general | solution.py:62
  160.9 23.1 %fusion = bf16[24,1536]{1,0:T(8,128)(2,1)S(1)} fusion(bf16[176,1536]{1,0:T(8,128)(2,1)S(1)} %convolution_convert_fusion.1), kind=kCustom, calls=%all-reduce-scatter | all-reduce-scatter fusion | flops 294913 | bytes 615424
  184.1 3.4 %collective-permute-start.2 = (bf16[14,1536]{1,0:T(8,128)(2,1)S(1)}, bf16[14,1536]{1,0:T(8,128)(2,1)S(1)}, u32[]{:S(2)}, u32[]{:S(2)}) collective-permute-start(bf16[14,1536]{1,0:T(8,128)(2,1)S(1)} %slice.380), channel_id=1, source_target_pairs={{0,1},{1,2},{2,3},{3,4},{4,5},{5,6},{6,7},{8,9},{9,10},{10,11},{11... | collective-permute-start | bytes 129032
  187.6 0.6 dynamic-slice.8
  188.8 3.4 %collective-permute-done.2 = bf16[14,1536]{1,0:T(8,128)(2,1)S(1)} collective-permute-done((bf16[14,1536]{1,0:T(8,128)(2,1)S(1)}, bf16[14,1536]{1,0:T(8,128)(2,1)S(1)}, u32[]{:S(2)}, u32[]{:S(2)}) %collective-permute-start.2) | collective-permute-done | bytes 43040
  192.4 29.3 %all-gather.1 = bf16[8,22,1536]{2,1,0:T(8,128)(2,1)S(1)} all-gather(bf16[1,22,1536]{2,1,0:T(8,128)(2,1)S(1)} %fusion.60), channel_id=1, replica_groups=mesh['seq'=32,'mp'=8] {'mp'}, dimensions={0}, use_global_device_ids=true | all-gather | bytes 608256 | tf_op jit(solution)/shard_map/all_gather | solution.py:135
  222.5 1.6 fusion.10
  224.5 1.9 collective-permute-start
  226.5 6.7 %collective-permute-start.1 = (bf16[15,192]{1,0:T(8,128)(2,1)S(1)}, bf16[15,192]{1,0:T(8,128)(2,1)S(1)}, u32[]{:S(2)}, u32[]{:S(2)}) collective-permute-start(bf16[15,192]{1,0:T(8,128)(2,1)S(1)} %get-tuple-element.36), channel_id=1, source_target_pairs={{8,0},{16,8},{24,16},{32,24},{40,32},{48,40},{56,48},{64,56},{72,6... | collective-permute-start | bytes 17288 | tf_op jit(solution)/shard_map/ppermute | solution.py:20
  233.2 1.3 collective-permute-done.1
  234.5 1.0 convolution_convert_fusion
  235.5 21.8 %fusion.1 = bf16[24,1536]{1,0:T(8,128)(2,1)S(1)} fusion(bf16[176,1536]{1,0:T(8,128)(2,1)S(1)} %convolution_convert_fusion), kind=kCustom, calls=%all-reduce-scatter.1 | all-reduce-scatter fusion | flops 294913 | bytes 615424
  257.4 2.0 collective-permute-start.3
  259.3 6.1 %collective-permute-done.3 = bf16[14,1536]{1,0:T(8,128)(2,1)S(1)} collective-permute-done((bf16[14,1536]{1,0:T(8,128)(2,1)S(1)}, bf16[14,1536]{1,0:T(8,128)(2,1)S(1)}, u32[]{:S(2)}, u32[]{:S(2)}) %collective-permute-start.3) | collective-permute-done | bytes 43040
  265.6 0.7 add_convert_fusion.4
  (63 shorter events, 4.5 us)
Async XLA Ops:
  6.5 154.1 %copy-start = (bf16[192,1536]{1,0:T(8,128)(2,1)S(1)}, bf16[192,1536]{1,0:T(8,128)(2,1)}, u32[]{:S(2)}) copy-start(bf16[192,1536]{1,0:T(8,128)(2,1)} %param.16) | copy-start | bytes 1769476
  6.5 91.7 %all-gather.5.cloned.1.call-start = ((), (), s32[]{:S(2)}) async-start(), calls=%async_computation | async-start | bytes 2973696 | tf_op jit(solution)/shard_map/all_gather | solution.py:123
  36.7 1.6 copy-start.4
  36.7 1.6 copy-start.5
  40.7 114.2 %all-gather.7.cloned.1.call-start = ((), (), s32[]{:S(2)}) async-start(), calls=%async_computation.1 | async-start | bytes 2973696 | tf_op jit(solution)/shard_map/all_gather | solution.py:124
  101.4 3.1 %copy-start.1 = (f32[176,2,5632]{2,0,1:T(8,128)}, f32[176,2,5632]{2,0,1:T(8,128)S(1)}, u32[]{:S(2)}) copy-start(f32[176,2,5632]{2,0,1:T(8,128)S(1)} %get-tuple-element.73) | copy-start | bytes 23789572
  160.5 27.0 %copy-start.3 = (f32[31,192]{1,0:T(8,128)S(1)}, f32[31,192]{1,0:T(8,128)}, u32[]{:S(2)}) copy-start(f32[31,192]{1,0:T(8,128)} %param.20) | copy-start | bytes 71428
  160.5 27.1 %copy-start.6 = (u32[256]{0:T(256)S(1)}, u32[256]{0:T(256)}, u32[]{:S(2)}) copy-start(u32[256]{0:T(256)} %constant.48) | copy-start | bytes 3076
  160.6 31.8 %copy-start.2 = (bf16[22,1536]{1,0:T(8,128)(2,1)S(1)}, bf16[22,1536]{1,0:T(8,128)(2,1)}, u32[]{:S(2)}) copy-start(bf16[22,1536]{1,0:T(8,128)(2,1)} %param.12) | copy-start | bytes 202756
  184.1 8.1 %collective-permute-start.2 = (bf16[14,1536]{1,0:T(8,128)(2,1)S(1)}, bf16[14,1536]{1,0:T(8,128)(2,1)S(1)}, u32[]{:S(2)}, u32[]{:S(2)}) collective-permute-start(bf16[14,1536]{1,0:T(8,128)(2,1)S(1)} %slice.380), channel_id=1, source_target_pairs={{0,1},{1,2},{2,3},{3,4},{4,5},{5,6},{6,7},{8,9},{9,10},{10,11},{11... | collective-permute-start | bytes 129032
  221.8 0.7 copy-start.9
  221.8 0.7 copy-start.10
  222.5 1.6 copy-start.7
  224.1 10.4 %copy-start.8 = (bf16[192,1536]{1,0:T(8,128)(2,1)S(1)}, bf16[192,1536]{1,0:T(8,128)(2,1)}, u32[]{:S(2)}) copy-start(bf16[192,1536]{1,0:T(8,128)(2,1)} %param.23) | copy-start | bytes 1769476
  224.1 10.4 %copy-start.11 = (f32[192]{0:T(256)S(1)}, f32[192]{0:T(256)}, u32[]{:S(2)}) copy-start(f32[192]{0:T(256)} %param.22) | copy-start | bytes 2308
  224.1 10.3 %copy-start.12 = (f32[192]{0:T(256)S(1)}, f32[192]{0:T(256)}, u32[]{:S(2)}) copy-start(f32[192]{0:T(256)} %param.21) | copy-start | bytes 2308
  224.5 8.6 %collective-permute-start = (bf16[15,192]{1,0:T(8,128)(2,1)S(1)}, bf16[15,192]{1,0:T(8,128)(2,1)S(1)}, u32[]{:S(2)}, u32[]{:S(2)}) collective-permute-start(bf16[15,192]{1,0:T(8,128)(2,1)S(1)} %get-tuple-element.35), channel_id=1, source_target_pairs={{0,8},{8,16},{16,24},{24,32},{32,40},{40,48},{48,56},{56,64},{64,7... | collective-permute-start | bytes 17288 | tf_op jit(solution)/shard_map/ppermute | solution.py:18
  226.5 8.0 %collective-permute-start.1 = (bf16[15,192]{1,0:T(8,128)(2,1)S(1)}, bf16[15,192]{1,0:T(8,128)(2,1)S(1)}, u32[]{:S(2)}, u32[]{:S(2)}) collective-permute-start(bf16[15,192]{1,0:T(8,128)(2,1)S(1)} %get-tuple-element.36), channel_id=1, source_target_pairs={{8,0},{16,8},{24,16},{32,24},{40,32},{48,40},{56,48},{64,56},{72,6... | collective-permute-start | bytes 17288 | tf_op jit(solution)/shard_map/ppermute | solution.py:20
  257.4 8.1 %collective-permute-start.3 = (bf16[14,1536]{1,0:T(8,128)(2,1)S(1)}, bf16[14,1536]{1,0:T(8,128)(2,1)S(1)}, u32[]{:S(2)}, u32[]{:S(2)}) collective-permute-start(bf16[14,1536]{1,0:T(8,128)(2,1)S(1)} %slice.381), channel_id=1, source_target_pairs={{0,1},{1,2},{2,3},{3,4},{4,5},{5,6},{6,7},{8,9},{9,10},{10,11},{11... | collective-permute-start | bytes 129032
Sparse Core Ops, SparseCore 0:
  40.8 57.3 all-gather.4
  100.9 54.0 all-gather.6
where the time goes:
time: 274 us; the launch traced here: 273 us
  waiting for transfers between devices  118 us (43%)
  blocking collectives  104 us (38%)
  between operations  14.5 us (5%)
  starting transfers between devices  14 us (5%)
  matrix products  13.6 us (5%)
  local copies, waits for them, and re-layouts  5.21 us (2%)
  other arithmetic  4.42 us (2%)
    all_gather x1, waiting for transfers between devices, local(): lax.all_gather(keys, 'seq', axis=0, tiled=True)  56.4 us
    all_gather x1, waiting for transfers between devices, local(): lax.all_gather(values, 'seq', axis=0, tiled=True)  50.5 us
    unnamed x2, blocking collectives  44.9 us
    all_gather x1, blocking collectives, local(): whole_in = lax.all_gather(frames_in, 'mp', axis=0, tiled=True)  29.5 us
    all_gather x1, blocking collectives, local(): whole_mid = lax.all_gather(mid, 'mp', axis=0, tiled=True)  29.3 us
    unnamed x4, waiting for transfers between devices  9.55 us
    ppermute x1, starting transfers between devices, padded_2(): lax.ppermute(head, axis, [((i + 1) % count, i) for i in range(ends)])  6.65 us
  transfers between devices with their start and end apart: 6, of which 5 were waited for; matrix products, arithmetic and copies ran while one was open for 2% of the time, Pallas kernels for 0%

commit v1 on v0

--- a/solution.py
+++ b/solution.py
@@ -121,7 +121,9 @@
         start_state,
         queries,
         lax.all_gather(keys, "seq", axis=0, tiled=True),
-        lax.all_gather(values, "seq", axis=0, tiled=True),
+        jnp.concatenate(
+            lax.all_to_all(jnp.stack([values] * lax.axis_size("seq")), "seq", 0, 0), axis=0
+        ),
         scale,
     )
     context = (

time: 274 us -> 260 us (0.949)
  waiting for transfers between devices: 118 us -> 85.2 us
  local copies, waits for them, and re-layouts: 5.21 us -> 18 us
  starting transfers between devices: 14 us -> 19.6 us
    all_to_all x0 -> x1, waiting for transfers between devices: none -> 69.4 us  [local(): lax.all_to_all(jnp.stack([values] * lax.axis_size('seq')), 'seq', 0, 0)]
    all_gather x1, waiting for transfers between devices: 56.4 us -> 0.02 us  [local(): lax.all_gather(keys, 'seq', axis=0, tiled=True)]
    all_gather x1 -> x0, waiting for transfers between devices: 50.5 us -> none  [local(): lax.all_gather(values, 'seq', axis=0, tiled=True)]
    all_to_all x0 -> x1, starting transfers between devices: none -> 10.6 us  [local(): lax.all_to_all(jnp.stack([values] * lax.axis_size('seq')), 'seq', 0, 0)]
    squeeze x0 -> x1, local copies, waits for them, and re-layouts: none -> 5.67 us  [attend(): result, unused = lax.scan(step, carry, (key_steps, value_steps))]
    ppermute x1, waiting for transfers between devices: 0.01 us -> 5.53 us  [padded_2(): lax.ppermute(tail, axis, [(i, (i + 1) % count) for i in range(ends)])]
    all_to_all x0 -> x1, local copies, waits for them, and re-layouts: none -> 5.25 us  [local(): lax.all_to_all(jnp.stack([values] * lax.axis_size('seq')), 'seq', 0, 0)]
    ppermute x1, starting transfers between devices: 6.65 us -> 1.92 us  [padded_2(): lax.ppermute(head, axis, [((i + 1) % count, i) for i in range(ends)])]
  transfers between devices with their start and end apart: 6 -> 6, of which waited for: 5 -> 4; matrix products, arithmetic and copies ran while one was open for 2% -> 7% of each run, Pallas kernels for 0% -> 0%
where the time goes in v1:
time: 260 us; the launch traced here: 259 us
  blocking collectives  104 us (40%)
  waiting for transfers between devices  85.2 us (33%)
  starting transfers between devices  19.6 us (8%)
  local copies, waits for them, and re-layouts  18 us (7%)
  between operations  14.5 us (6%)
  matrix products  12.1 us (5%)
  other arithmetic  5.07 us (2%)
    all_to_all x1, waiting for transfers between devices, local(): lax.all_to_all(jnp.stack([values] * lax.axis_size('seq')), 'seq', 0, 0)  69.4 us
    unnamed x2, blocking collectives  45.5 us
    all_gather x1, blocking collectives, local(): whole_in = lax.all_gather(frames_in, 'mp', axis=0, tiled=True)  29.5 us
    all_gather x1, blocking collectives, local(): whole_mid = lax.all_gather(mid, 'mp', axis=0, tiled=True)  29.1 us
    all_to_all x1, starting transfers between devices, local(): lax.all_to_all(jnp.stack([values] * lax.axis_size('seq')), 'seq', 0, 0)  10.6 us
    unnamed x3, waiting for transfers between devices  10.3 us
    dot_general x5, matrix products, project_out_in(): lax.dot_general(inputs, weight, (((1,), (1,)), ((), ())), preferred_eleme...  6.18 us
    squeeze x1, local copies, waits for them, and re-layouts, attend(): result, unused = lax.scan(step, carry, (key_steps, value_steps))  5.67 us
  transfers between devices with their start and end apart: 6, of which 4 were waited for; matrix products, arithmetic and copies ran while one was open for 7% of the time, Pallas kernels for 0%

profile of v1, /device:TPU:56, one launch (start us, length us, event | category | flops | bytes accessed | tf_op | source)
XLA Modules:
  0.0 258.6 jit_solution(9921146367573208520)
XLA Ops:
  6.5 29.5 %all-gather = bf16[8,22,1536]{2,1,0:T(8,128)(2,1)S(1)} all-gather(bf16[1,22,1536]{2,1,0:T(8,128)(2,1)} %bitcast.78), channel_id=1, replica_groups=mesh['seq'=32,'mp'=8] {'mp'}, dimensions={0}, use_global_device_ids=true | all-gather | bytes 608256 | tf_op jit(solution)/shard_map/all_gather | solution.py:104
  36.7 2.6 fusion.65
  40.7 2.0 stack.2
  42.7 10.6 %all-to-all-start = ((bf16[32,176,2,96]{3,1,2,0:T(8,128)(2,1)}), bf16[32,176,2,96]{3,1,2,0:T(8,128)(2,1)S(1)}, u32[]{:S(2)}, u32[]{:S(2)}) async-start(bf16[32,176,2,96]{3,1,2,0:T(8,128)(2,1)} %stack.2), calls=%async_computation | async-start | bytes 5767168 | tf_op jit(solution)/shard_map/all_to_all | solution.py:125
  53.4 2.3 fusion.71
  55.6 1.6 fusion.70
  59.3 69.4 %all-to-all-done = bf16[32,176,2,96]{3,1,2,0:T(8,128)(2,1)S(1)} async-done(((bf16[32,176,2,96]{3,1,2,0:T(8,128)(2,1)}), bf16[32,176,2,96]{3,1,2,0:T(8,128)(2,1)S(1)}, u32[]{:S(2)}, u32[]{:S(2)}) %all-to-all-start) | async-done | bytes 2162720 | tf_op jit(solution)/shard_map/all_to_all | solution.py:125
  128.6 5.2 %copy.16 = bf16[32,176,2,96]{1,0,3,2:T(8,128)(2,1)} copy(bf16[32,176,2,96]{3,1,2,0:T(8,128)(2,1)S(1)} %all-to-all-done) | data formatting | bytes 4325376 | tf_op jit(solution)/shard_map/all_to_all | solution.py:125
  133.9 5.7 %squeeze.16 = bf16[5632,2,96]{0,2,1:T(8,128)(2,1)S(1)} reshape(bf16[32,176,2,96]{1,0,3,2:T(8,128)(2,1)} %copy.16) | data formatting | bytes 4325376 | tf_op jit(solution)/shard_map/while/body/jit(dynamic_index_in_dim)/squeeze | solution.py:82
  139.6 3.1 %fusion.69 = (f32[176,2]{0,1:T(2,128)S(1)}, f32[176,2,5632]{2,0,1:T(8,128)S(1)}) fusion(bf16[5632,2,96]{2,0,1:T(8,128)(2,1)} %all-gather.4.cloned.1.call-done, bf16[176,2,48]{2,0,1:T(8,128)(2,1)S(1)} %copy-done.5, bf16[176,2,48]{2,0,1:T(8,128)(2,1)S(1)} %copy-done.4), kind=kOutput, calls=%fused_computation.138 | convolution fusion | flops 384732832 | bytes 10161536 | tf_op jit(solution)/shard_map/while/body/eval_jaxpr/qhd,khd->qhk/dot_general | solution.py:56
  142.8 1.2 fusion.3
  144.0 1.4 fusion.21
  146.0 23.3 %fusion = bf16[24,1536]{1,0:T(8,128)(2,1)S(1)} fusion(bf16[176,1536]{1,0:T(8,128)(2,1)S(1)} %convolution_convert_fusion.1), kind=kCustom, calls=%all-reduce-scatter | all-reduce-scatter fusion | flops 294913 | bytes 615424
  169.3 2.4 collective-permute-start.2
  173.0 4.4 %collective-permute-done.2 = bf16[14,1536]{1,0:T(8,128)(2,1)S(1)} collective-permute-done((bf16[14,1536]{1,0:T(8,128)(2,1)S(1)}, bf16[14,1536]{1,0:T(8,128)(2,1)S(1)}, u32[]{:S(2)}, u32[]{:S(2)}) %collective-permute-start.2) | collective-permute-done | bytes 43040
  177.6 29.1 %all-gather.1 = bf16[8,22,1536]{2,1,0:T(8,128)(2,1)S(1)} all-gather(bf16[1,22,1536]{2,1,0:T(8,128)(2,1)S(1)} %fusion.60), channel_id=1, replica_groups=mesh['seq'=32,'mp'=8] {'mp'}, dimensions={0}, use_global_device_ids=true | all-gather | bytes 608256 | tf_op jit(solution)/shard_map/all_gather | solution.py:137
  207.6 1.5 fusion.13
  209.6 1.9 collective-permute-start.1
  211.5 2.4 collective-permute-start
  214.0 5.5 %collective-permute-done = bf16[15,192]{1,0:T(8,128)(2,1)S(1)} collective-permute-done((bf16[15,192]{1,0:T(8,128)(2,1)S(1)}, bf16[15,192]{1,0:T(8,128)(2,1)S(1)}, u32[]{:S(2)}, u32[]{:S(2)}) %collective-permute-start) | collective-permute-done | bytes 5792 | tf_op jit(solution)/shard_map/ppermute | solution.py:18
  219.5 1.1 convolution_convert_fusion
  220.6 22.2 %fusion.1 = bf16[24,1536]{1,0:T(8,128)(2,1)S(1)} fusion(bf16[176,1536]{1,0:T(8,128)(2,1)S(1)} %convolution_convert_fusion), kind=kCustom, calls=%all-reduce-scatter.1 | all-reduce-scatter fusion | flops 294913 | bytes 615424
  242.8 2.2 collective-permute-start.3
  245.0 5.9 %collective-permute-done.3 = bf16[14,1536]{1,0:T(8,128)(2,1)S(1)} collective-permute-done((bf16[14,1536]{1,0:T(8,128)(2,1)S(1)}, bf16[14,1536]{1,0:T(8,128)(2,1)S(1)}, u32[]{:S(2)}, u32[]{:S(2)}) %collective-permute-start.3) | collective-permute-done | bytes 43040
  (71 shorter events, 7.6 us)
Async XLA Ops:
  6.5 139.1 %copy-start = (bf16[192,1536]{1,0:T(8,128)(2,1)S(1)}, bf16[192,1536]{1,0:T(8,128)(2,1)}, u32[]{:S(2)}) copy-start(bf16[192,1536]{1,0:T(8,128)(2,1)} %param.16) | copy-start | bytes 1769476
  36.7 2.6 %copy-start.7 = (f32[1536]{0:T(1024)S(1)}, f32[1536]{0:T(1024)}, u32[]{:S(2)}) copy-start(f32[1536]{0:T(1024)} %param.14) | copy-start | bytes 18436
  36.7 2.6 copy-start.8
  39.6 0.8 copy-start.1
  42.7 85.9 %all-to-all-start = ((bf16[32,176,2,96]{3,1,2,0:T(8,128)(2,1)}), bf16[32,176,2,96]{3,1,2,0:T(8,128)(2,1)S(1)}, u32[]{:S(2)}, u32[]{:S(2)}) async-start(bf16[32,176,2,96]{3,1,2,0:T(8,128)(2,1)} %stack.2), calls=%async_computation | async-start | bytes 5767168 | tf_op jit(solution)/shard_map/all_to_all | solution.py:125
  53.3 86.3 %all-gather.4.cloned.1.call-start = ((), (), s32[]{:S(2)}) async-start(), calls=%async_computation.1 | async-start | bytes 2973696 | tf_op jit(solution)/shard_map/all_gather | solution.py:123
  55.6 2.0 copy-start.2
  133.9 5.7 %copy-start.4 = (bf16[176,2,48]{2,0,1:T(8,128)(2,1)S(1)}, bf16[176,2,48]{2,0,1:T(8,128)(2,1)}, u32[]{:S(2)}) copy-start(bf16[176,2,48]{2,0,1:T(8,128)(2,1)} %get-tuple-element.20) | copy-start | bytes 101380
  133.9 5.7 %copy-start.5 = (bf16[176,2,48]{2,0,1:T(8,128)(2,1)S(1)}, bf16[176,2,48]{2,0,1:T(8,128)(2,1)}, u32[]{:S(2)}) copy-start(bf16[176,2,48]{2,0,1:T(8,128)(2,1)} %get-tuple-element.28) | copy-start | bytes 101380
  145.5 26.2 %copy-start.6 = (f32[31,192]{1,0:T(8,128)S(1)}, f32[31,192]{1,0:T(8,128)}, u32[]{:S(2)}) copy-start(f32[31,192]{1,0:T(8,128)} %param.20) | copy-start | bytes 71428
  145.5 26.3 %copy-start.9 = (u32[256]{0:T(256)S(1)}, u32[256]{0:T(256)}, u32[]{:S(2)}) copy-start(u32[256]{0:T(256)} %constant.48) | copy-start | bytes 3076
  145.7 31.9 %copy-start.3 = (bf16[22,1536]{1,0:T(8,128)(2,1)S(1)}, bf16[22,1536]{1,0:T(8,128)(2,1)}, u32[]{:S(2)}) copy-start(bf16[22,1536]{1,0:T(8,128)(2,1)} %param.12) | copy-start | bytes 202756
  169.3 8.1 %collective-permute-start.2 = (bf16[14,1536]{1,0:T(8,128)(2,1)S(1)}, bf16[14,1536]{1,0:T(8,128)(2,1)S(1)}, u32[]{:S(2)}, u32[]{:S(2)}) collective-permute-start(bf16[14,1536]{1,0:T(8,128)(2,1)S(1)} %slice.380), channel_id=1, source_target_pairs={{0,1},{1,2},{2,3},{3,4},{4,5},{5,6},{6,7},{8,9},{9,10},{10,11},{11... | collective-permute-start | bytes 129032
  206.9 0.7 copy-start.12
  206.9 0.7 copy-start.13
  207.6 1.6 copy-start.10
  209.2 10.3 %copy-start.11 = (bf16[192,1536]{1,0:T(8,128)(2,1)S(1)}, bf16[192,1536]{1,0:T(8,128)(2,1)}, u32[]{:S(2)}) copy-start(bf16[192,1536]{1,0:T(8,128)(2,1)} %param.23) | copy-start | bytes 1769476
  209.2 10.3 %copy-start.14 = (f32[192]{0:T(256)S(1)}, f32[192]{0:T(256)}, u32[]{:S(2)}) copy-start(f32[192]{0:T(256)} %param.22) | copy-start | bytes 2308
  209.2 10.3 %copy-start.15 = (f32[192]{0:T(256)S(1)}, f32[192]{0:T(256)}, u32[]{:S(2)}) copy-start(f32[192]{0:T(256)} %param.21) | copy-start | bytes 2308
  209.6 4.4 %collective-permute-start.1 = (bf16[15,192]{1,0:T(8,128)(2,1)S(1)}, bf16[15,192]{1,0:T(8,128)(2,1)S(1)}, u32[]{:S(2)}, u32[]{:S(2)}) collective-permute-start(bf16[15,192]{1,0:T(8,128)(2,1)S(1)} %get-tuple-element.36), channel_id=1, source_target_pairs={{8,0},{16,8},{24,16},{32,24},{40,32},{48,40},{56,48},{64,56},{72,6... | collective-permute-start | bytes 17288 | tf_op jit(solution)/shard_map/ppermute | solution.py:20
  211.5 8.0 %collective-permute-start = (bf16[15,192]{1,0:T(8,128)(2,1)S(1)}, bf16[15,192]{1,0:T(8,128)(2,1)S(1)}, u32[]{:S(2)}, u32[]{:S(2)}) collective-permute-start(bf16[15,192]{1,0:T(8,128)(2,1)S(1)} %get-tuple-element.35), channel_id=1, source_target_pairs={{0,8},{8,16},{16,24},{24,32},{32,40},{40,48},{48,56},{56,64},{64,7... | collective-permute-start | bytes 17288 | tf_op jit(solution)/shard_map/ppermute | solution.py:18
  242.8 8.1 %collective-permute-start.3 = (bf16[14,1536]{1,0:T(8,128)(2,1)S(1)}, bf16[14,1536]{1,0:T(8,128)(2,1)S(1)}, u32[]{:S(2)}, u32[]{:S(2)}) collective-permute-start(bf16[14,1536]{1,0:T(8,128)(2,1)S(1)} %slice.381), channel_id=1, source_target_pairs={{0,1},{1,2},{2,3},{3,4},{4,5},{5,6},{6,7},{8,9},{9,10},{10,11},{11... | collective-permute-start | bytes 129032
Sparse Core Ops, SparseCore 0:
  59.4 77.7 all-gather.3
